TPU v7x, 128 devices: a whole 4x4x4 slice. The times are simulated.
128 devices in a mesh: blk: 32 (over z, y, core), rep: 4 (over x).
Axes of the slice: x: 4, y: 4, z: 4, core: 2. Of those that a mesh axis runs over, the one named last changes fastest.
Arguments:
- tiles: bfloat16 [4, 1024, 128, 128], P('rep', 'blk'), may hold values from -6 to 6
- tile_rows: int32 [4, 1024], P('rep', 'blk'), may hold values from 1 to 128
- tile_owner: int32 [4, 1024, 1], P('rep', 'blk'), may hold values from 0 to 31; in each aligned block of 32 rows (0 to 31, 32 to 63, ..., all dimensions but the last counted through in order) at most 2 rows name the same one
- tile_slot: int32 [4, 1024], P('rep', 'blk'), may hold values from 0 to 15
- neighbors: int32 [4, 128, 27], P('rep', 'blk'), may hold values from -1 to 11, as said below
- w_enc: bfloat16 [27, 128, 128], replicated, may hold values from -0.109375 to 0.109375
- w_coarse: bfloat16 [128, 128], replicated, may hold values from -0.5 to 0.5
- w_dec: bfloat16 [27, 128, 128], replicated, may hold values from -0.109375 to 0.109375
- cotangent: bfloat16 [4, 128, 512, 128], P('rep', 'blk'), may hold values from -0.01171875 to 0.01171875
Outputs:
- decoded: bfloat16 [4, 128, 512, 128], P('rep', 'blk')
- weight_grad: float32 [27, 128, 128], replicated
Inputs may be any that keep to these rules, and one draw needn't show every extreme that they name: `tile_owner`: among the tiles of one index of blk, no owner is named by more than 2; some owner is named by exactly 2. `neighbors`: entry 13 of block g is 4 + g % 4. An entry e >= 0 names block e of the three consecutive blk indices index - 1, index, index + 1 laid end to end; -1 means no active neighbour.
All inputs are finite; a program needn't handle non-finite values.
Results may differ from a plain program's by a relative error of at most 0.013.
Values may be sent and summed in bfloat16 or wider, within the bound.
A program may use at most 64 MiB of HBM per device.

v0:
```python
import functools
import math

import jax
import jax.numpy as jnp
from jax import lax
from jax.experimental import pallas as pl
from jax.experimental.pallas import tpu as pltpu
from jax.sharding import PartitionSpec as P

C = 128
CAP = 2
BLK = 4
SIB = 4
F32 = jnp.float32
BF16 = jnp.bfloat16
MESH = pl.DeviceIdType.MESH
WINDOW = 16
VMEM_LIMIT = 48 * 1024 * 1024


def at_blk(index):
    return {"blk": index}


def at_rep(index):
    return {"rep": index}


def fill_weights(w_ref, big):
    zero = jnp.zeros((C, C), BF16)
    for u in range(4):
        for dy in range(3):
            for dz in range(3):
                for half in range(2):
                    dx = u - half
                    tap = w_ref[dx * 9 + dy * 3 + dz] if 0 <= dx <= 2 else zero
                    big[u * 3 + dy, dz * C : dz * C + C, half * C : half * C + C] = tap


def fill_shifts(tab_ref, field, shifts):
    level = lax.broadcasted_iota(jnp.int32, (10, 8, C), 1)

    def body(i, carry):
        pair, plane = i // 10, i % 10
        first = jnp.where(plane == 0, 0, jnp.where(plane == 9, 2, 1))
        at = lax.rem(plane + 7, 8)
        parts = []
        for j in range(2):
            base = (2 * pair + j) * 27 + first * 9
            cells = []
            for c in range(3):
                low = field[tab_ref[base + c], at, 48:64].astype(F32)[8:16]
                mid = field[tab_ref[base + 3 + c], at].astype(F32)
                high = field[tab_ref[base + 6 + c], at, 0:16].astype(F32)[0:8]
                cells.append(jnp.concatenate([low, mid, high], axis=0).reshape(10, 8, C))
            parts.append(
                (
                    pltpu.roll(jnp.where(level == 7, cells[0], cells[1]), 1, 1),
                    cells[1],
                    pltpu.roll(jnp.where(level == 0, cells[2], cells[1]), 7, 1),
                )
            )
        for c in range(3):
            both = jnp.concatenate([parts[0][c], parts[1][c]], axis=1).astype(BF16)
            shifts[pair, lax.rem(plane, 2), plane // 2, :, :, c * C : c * C + C] = both
        return carry

    lax.fori_loop(0, 20, body, 0)


def operand(shifts, pair, u, dy):
    return shifts[pair, u % 2, u // 2 : u // 2 + 4, dy : dy + 8].reshape(512, 3 * C)


def convolve(shifts, big, pair):
    taps = [operand(shifts, pair, u, dy) for u in range(4) for dy in range(3)]
    total = jnp.dot(
        jnp.concatenate(taps, axis=1),
        big[...].reshape(36 * C, 2 * C),
        preferred_element_type=F32,
    )
    return total.reshape(4, 8, 2, 8, 2 * C)


def kernel(
    count,
    peers,
    reps,
    rows_hbm,
    owner_hbm,
    slot_hbm,
    neighbors_hbm,
    tiles_hbm,
    wenc_hbm,
    wcoarse_ref,
    wdec_hbm,
    cot_hbm,
    dec_ref,
    grad_ref,
    rows_s,
    owner_s,
    slot_s,
    neighbors_s,
    table_s,
    places_v,
    places_s,
    tiles,
    outgoing,
    outgoing_label,
    arrived,
    arrived_label,
    landed,
    field,
    encoded,
    shifts,
    big,
    big2,
    wenc,
    wdec,
    cot,
    cot_t,
    pooled,
    means,
    part,
    half_in,
    half,
    piece_in,
    piece_x,
    piece_own,
    ends,
    ends_in,
    ends2,
    ends2_in,
    load_sems,
    tile_sems,
    label_sems,
    halo_sems,
    encoded_sems,
    sibling_sems,
    mean_sems,
    core_sems,
    plane_sems,
    x_sems,
    gather_sems,
    forward_sems,
):
    me = lax.axis_index("blk")
    rep = lax.axis_index("rep")
    chips = peers // 2
    side = math.isqrt(chips)
    core, chip = lax.rem(me, 2), me // 2
    chip_y, chip_z = lax.rem(chip, side), chip // side
    other = me + 1 - 2 * core
    right, left = lax.rem(me + 1, peers), lax.rem(me + peers - 1, peers)

    loads = [
        pltpu.make_async_copy(source, target, load_sems.at[i])
        for i, (source, target) in enumerate(
            [
                (owner_hbm, owner_s),
                (rows_hbm, rows_s),
                (slot_hbm, slot_s),
                (tiles_hbm, tiles),
                (neighbors_hbm, neighbors_s),
                (wenc_hbm, wenc),
                (wdec_hbm, wdec),
                (cot_hbm, cot),
            ]
        )
    ]
    for load in loads:
        load.start()

    def remote(source, target, send_sem, recv_sem, where):
        return pltpu.make_async_remote_copy(
            src_ref=source,
            dst_ref=target,
            send_sem=send_sem,
            recv_sem=recv_sem,
            device_id=where,
            device_id_type=MESH,
        )

    def drain(ref, sem):
        pltpu.make_async_copy(ref, ref, sem).wait()

    turn = lax.rem(me, SIB)
    across = me - turn + lax.rem(turn + 2, SIB)

    def plane_peer(step):
        return 2 * lax.rem(chip + step, chips) + core

    def rep_peer(step):
        return lax.rem(rep + step, reps)

    barrier = pltpu.get_barrier_semaphore()

    def greet(step, carry):
        pl.semaphore_signal(
            barrier, inc=1, device_id=at_blk(lax.rem(me + step, peers)), device_id_type=MESH
        )
        return carry

    lax.fori_loop(1, peers, greet, 0)
    for step in range(1, reps):
        pl.semaphore_signal(
            barrier, inc=1, device_id=at_rep(rep_peer(step)), device_id_type=MESH
        )

    loads[0].wait()
    lane = lax.broadcasted_iota(jnp.int32, (8, C), 1)

    def note(t, carry):
        first, second = carry
        hit = lane == owner_s[0, t]
        second = jnp.where(hit & (first >= 0), t, second)
        first = jnp.where(hit & (first < 0), t, first)
        return first, second

    none = jnp.full((8, C), -1, jnp.int32)
    first, second = lax.fori_loop(0, count, note, (none, none))
    places_v[...] = jnp.where(lax.broadcasted_iota(jnp.int32, (8, C), 0) == 0, first, second)
    move = pltpu.make_async_copy(places_v, places_s, load_sems.at[8])
    move.start()
    loads[1].wait()
    loads[2].wait()
    move.wait()
    loads[3].wait()
    row = lax.broadcasted_iota(jnp.int32, (C, C), 0)

    def bucket(owner):
        for rank in range(CAP):
            tile = places_s[rank, owner]
            at = jnp.maximum(tile, 0)
            live = jnp.where(tile >= 0, rows_s[0, at], 0)
            outgoing[owner, rank] = jnp.where(row < live, tiles[at].astype(F32), 0.0).astype(BF16)
            outgoing_label[owner, rank : rank + 1] = jnp.full((1, C), slot_s[0, at], jnp.int32)

    def chip_beside(step, sign):
        k = step // 2
        move_y = lax.rem(k, side)
        move_z = lax.rem(k // side + move_y, side)
        return side * lax.rem(chip_z + side + sign * move_z, side) + lax.rem(
            chip_y + side + sign * move_y, side
        )

    def target_of(step):
        return 2 * chip_beside(step, 1 - 2 * core) + lax.rem(core + step, 2)

    def source_of(step):
        from_core = lax.rem(core + step, 2)
        return 2 * chip_beside(step, 2 * from_core - 1) + from_core

    def label_move(step):
        peer = target_of(step)
        return remote(
            outgoing_label.at[peer],
            arrived_label.at[me],
            label_sems.at[0],
            label_sems.at[step],
            at_blk(peer),
        )

    def tile_move(step):
        peer = target_of(step)
        return remote(
            outgoing.at[peer], arrived.at[me], tile_sems.at[0], tile_sems.at[step], at_blk(peer)
        )

    pl.semaphore_wait(barrier, peers - 1 + reps - 1)

    def step_of(i):
        return 1 + lax.rem(i + 1, peers - 1)

    def send(i, carry):
        step = step_of(i)
        bucket(target_of(step))
        label_move(step).start()
        tile_move(step).start()
        return carry

    lax.fori_loop(0, WINDOW, send, 0)
    bucket(me)

    landed[...] = jnp.zeros_like(landed)

    def land(labels, tiles_at):
        rows = [labels[rank : rank + 1] for rank in range(CAP)]
        for at in range(0, C, 32):
            pieces = [tiles_at[rank, at : at + 32].astype(F32) for rank in range(CAP)]
            for quarter in range(4 * BLK):
                total = landed[quarter, at : at + 32]
                for rank in range(CAP):
                    total = total + jnp.where(rows[rank] == quarter, pieces[rank], 0.0)
                landed[quarter, at : at + 32] = total

    land(outgoing_label[me], outgoing.at[me])
    loads[4].wait()

    def look(block, carry):
        for column in range(27):
            entry = neighbors_s[block, column]
            beside = me + entry // BLK - 1
            keep = (entry >= 0) & (beside >= 0) & (beside < peers)
            table_s[block * 27 + column] = jnp.where(keep, entry, 3 * BLK)
        return carry

    lax.fori_loop(0, BLK, look, 0)
    field[3 * BLK] = jnp.zeros((8, 64, C), BF16)
    loads[5].wait()
    fill_weights(wenc, big)
    loads[6].wait()
    fill_weights(wdec, big2)
    loads[7].wait()
    for pair in range(2):
        for parity in range(2):
            for xh in range(4):
                rows = [
                    cot[2 * pair + j, parity + 2 * xh].astype(F32).reshape(8, 1, 8, C)
                    for j in range(2)
                ]
                rows = jnp.concatenate(rows, axis=1).reshape(128, C)
                at = pair * 512 + xh * 128
                cot_t[parity * C : parity * C + C, at : at + 128] = rows.T.astype(BF16)

    def arrive(i, carry):
        step = step_of(i)
        source = source_of(step)
        drain(arrived.at[source], tile_sems.at[step])
        drain(arrived_label.at[source], label_sems.at[step])

        @pl.when(i + WINDOW < peers - 1)
        def _():
            send(i + WINDOW, 0)

        land(arrived_label[source], arrived.at[source])
        return carry

    lax.fori_loop(0, peers - 1, arrive, 0)
    for quarter in range(4 * BLK):
        planes = landed[quarter].astype(BF16).reshape(2, 64, C)
        x = 2 * (quarter % 4)
        field[BLK + quarter // 4, x : x + 2] = planes

    sub_row = lax.broadcasted_iota(jnp.int32, (8, C), 0)

    def pack_ends(source, block, ends):
        packed = []
        for x in range(1, 7):
            columns = source[BLK + block, x, 16:48].astype(F32).reshape(4, 8, C)
            total = columns[0]
            for i in range(4):
                total = jnp.where(sub_row == i, pltpu.roll(columns[i], i, 0), total)
                total = jnp.where(sub_row == 4 + i, pltpu.roll(columns[i], (i + 5) % 8, 0), total)
            packed.append(total)
        ends[block] = jnp.concatenate(packed, axis=0).astype(BF16)

    def unpack_ends(ends_in, target):
        def body(at, carry):
            side_of, block = at // BLK, lax.rem(at, BLK)
            packed = ends_in[side_of, block].astype(F32).reshape(6, 8, C)
            for x in range(1, 7):
                ends = packed[x - 1]
                columns = [
                    jnp.where(
                        sub_row == 7, pltpu.roll(ends, 3 - i, 0), pltpu.roll(ends, (8 - i) % 8, 0)
                    )
                    for i in range(4)
                ]
                target[2 * BLK * side_of + block, x, 16:48] = jnp.concatenate(
                    columns, axis=0
                ).astype(BF16)
            return carry

        lax.fori_loop(0, 2 * BLK, body, 0)

    def plane_moves(ref, first, count, sems):
        moves = []
        for base, where in ((0, right), (2 * BLK, left)):
            source, target = pl.ds(BLK + first, count), pl.ds(base + first, count)
            for x in (0, 7):
                moves.append(
                    remote(
                        ref.at[source, x], ref.at[target, x], sems.at[0], sems.at[1], at_blk(where)
                    )
                )
        return moves

    def row_moves(ref, sems):
        moves = []
        for base, where in ((0, right), (2 * BLK, left)):
            source, target = pl.ds(BLK, BLK), pl.ds(base, BLK)
            for y in (0, 48):
                at = pl.ds(y, 16)
                moves.append(
                    remote(
                        ref.at[source, 1:7, at],
                        ref.at[target, 1:7, at],
                        sems.at[2],
                        sems.at[3],
                        at_blk(where),
                    )
                )
        return moves

    def ends_moves(ends, ends_in, sems):
        return [
            remote(ends, ends_in.at[side_of], sems.at[4], sems.at[5], at_blk(where))
            for side_of, where in ((0, right), (1, left))
        ]

    def shell_drain(ref, ends_in, sems, which):
        drain(ref.at[0 : 2 * BLK, 0:2], sems.at[which])
        drain(ref.at[0 : 2 * BLK, 1:7, 0:32], sems.at[2 + which])
        drain(ends_in, sems.at[4 + which])

    for move in plane_moves(field, 0, BLK, halo_sems) + row_moves(field, halo_sems):
        move.start()

    def pack_own(block, carry):
        pack_ends(field, block, ends)
        return carry

    lax.fori_loop(0, BLK, pack_own, 0)
    for move in ends_moves(ends, ends_in, halo_sems):
        move.start()
    shell_drain(field, ends_in, halo_sems, 1)
    unpack_ends(ends_in, field)
    shell_drain(field, ends_in, halo_sems, 0)

    fill_shifts(table_s, field, shifts)
    level = lax.broadcasted_iota(jnp.int32, (8, C), 0)
    even = lax.rem(level, 2) == 0

    def sibling_move(pair, where, kind):
        piece = pooled.at[turn, pl.ds(2 * pair, 2)]
        return remote(
            piece, piece, sibling_sems.at[0], sibling_sems.at[1 + kind], at_blk(where)
        )

    def encode(pair, carry):
        total = convolve(shifts, big, pair)
        rounded = jnp.maximum(total, 0.0).astype(BF16).astype(F32)
        for j in range(2):
            for xh in range(4):
                for half_x in range(2):
                    encoded[BLK + 2 * pair + j, 2 * xh + half_x] = (
                        rounded[xh, :, j, :, half_x * C : half_x * C + C]
                        .reshape(64, C)
                        .astype(BF16)
                    )
                flat = rounded[xh, :, j, :, :C] + rounded[xh, :, j, :, C:]
                flat = flat.reshape(4, 2, 8, C)
                flat = flat[:, 0] + flat[:, 1]
                folded = [
                    flat[y]
                    + jnp.where(even, pltpu.roll(flat[y], 7, 0), pltpu.roll(flat[y], 1, 0))
                    for y in range(4)
                ]
                packed = [
                    jnp.where(even, folded[2 * y], folded[2 * y + 1]) * 0.125 for y in range(2)
                ]
                pooled[turn, 2 * pair + j, xh] = jnp.concatenate(packed, axis=0).astype(BF16)
        sibling_move(pair, across, pair).start()
        sibling_move(pair, other, 2).start()
        for move in plane_moves(encoded, 2 * pair, 2, encoded_sems):
            move.start()

        @pl.when(pair == 1)
        def _():
            for move in row_moves(encoded, encoded_sems):
                move.start()

        for j in range(2):
            pack_ends(encoded, 2 * pair + j, ends2)
        return carry

    lax.fori_loop(0, 2, encode, 0)
    for move in ends_moves(ends2, ends2_in, encoded_sems):
        move.start()

    opposite = lax.rem(turn + 2, SIB)
    for pair in range(2):
        piece = pooled.at[opposite, 2 * pair : 2 * pair + 2]
        drain(piece, sibling_sems.at[1 + pair])
        remote(piece, piece, sibling_sems.at[0], sibling_sems.at[4], at_blk(other)).start()
    drain(pooled.at[0], sibling_sems.at[3])
    drain(pooled.at[0], sibling_sems.at[4])
    mean = pooled[0].astype(F32)
    for step in range(1, SIB):
        mean = mean + pooled[step].astype(F32)
    means[1] = (mean * (1.0 / SIB)).astype(BF16)

    def mean_move(side_of, where):
        return remote(
            means.at[1], means.at[side_of], mean_sems.at[0], mean_sems.at[1], at_blk(where)
        )

    @pl.when(turn == SIB - 1)
    def _():
        mean_move(0, right).start()
        means[0] = means[1]

    @pl.when(turn == 0)
    def _():
        mean_move(2, left).start()
        means[2] = means[1]

    @pl.when((turn != 0) & (turn != SIB - 1))
    def _():
        means[0] = means[1]
        means[2] = means[1]

    def join(side_of):
        coarse = jnp.dot(
            means[side_of].reshape(BLK * 64, C), wcoarse_ref[...], preferred_element_type=F32
        )
        coarse = jnp.maximum(coarse, 0.0).reshape(BLK, 4, 2, 8, C)
        for block in range(BLK):
            for xh in range(4):
                ups = []
                for y in range(2):
                    tile = coarse[block, xh, y]
                    for up in (
                        jnp.where(even, tile, pltpu.roll(tile, 1, 0)),
                        jnp.where(even, pltpu.roll(tile, 7, 0), tile),
                    ):
                        ups += [up, up]
                ups = jnp.concatenate(ups, axis=0)
                for half_x in range(2):
                    x = 2 * xh + half_x
                    at = BLK * side_of + block
                    field[at, x] = (encoded[at, x].astype(F32) + ups).astype(BF16)

    join(1)

    @pl.when((turn == 0) | (turn == SIB - 1))
    def _():
        drain(means.at[1], mean_sems.at[0])
        drain(means.at[1], mean_sems.at[1])

    shell_drain(encoded, ends2_in, encoded_sems, 1)
    unpack_ends(ends2_in, encoded)
    join(0)
    join(2)
    fill_shifts(table_s, field, shifts)

    group_half = half_in.shape[1]
    piece_rows = piece_own.shape[1]
    active = group_half // piece_rows

    def swap(group):
        return remote(
            part.at[group, pl.ds(pl.multiple_of((1 - core) * group_half, 16), group_half)],
            half_in.at[group],
            core_sems.at[0],
            core_sems.at[1 + group],
            at_blk(other),
        )

    def piece_at(index):
        return pl.ds(pl.multiple_of(index * piece_rows, 16), piece_rows)

    def final_at(group, side_of, index):
        start = side_of * group_half + index * piece_rows
        start = start // (3 * C) * (9 * C) + group * (3 * C) + lax.rem(start, 3 * C)
        return pl.ds(pl.multiple_of(start, 16), piece_rows)

    def to_chip(step):
        return lax.rem(chip + step, chips)

    def from_chip(step):
        return lax.rem(chip + chips - step, chips)

    def scatter(group, step):
        return remote(
            half.at[group, piece_at(to_chip(step))],
            piece_in.at[group, chip],
            plane_sems.at[0],
            plane_sems.at[1 + group],
            at_blk(plane_peer(step)),
        )

    def gather(group, step):
        return remote(
            piece_own.at[group],
            grad_ref.at[final_at(group, core, chip)],
            gather_sems.at[0],
            gather_sems.at[1 + group if group < 2 else 2 + step],
            at_blk(plane_peer(step)),
        )

    def forward(group, index, source=None):
        at = final_at(group, core, index)
        return remote(
            grad_ref.at[at] if source is None else source,
            grad_ref.at[at], forward_sems.at[0],
            forward_sems.at[1],
            at_blk(other),

        )

    def each_step(action):
        def body(step, carry):
            action(step)
            return carry

        lax.fori_loop(1, chips, body, 0)

    def halve(group):
        drain(half_in.at[group], core_sems.at[1 + group])
        mine = pl.ds(pl.multiple_of(core * group_half, 16), group_half)
        half[group] = (part[group, mine].astype(F32) + half_in[group].astype(F32)).astype(BF16)

        def start(step):
            @pl.when(to_chip(step) < active)
            def _():
                scatter(group, step).start()

        each_step(start)

    def tap_row(dy, carry):
        @pl.when(dy < 3)
        def _():
            rows = [
                jnp.concatenate(
                    [
                        shifts[pair, u % 2, u // 2 : u // 2 + 4, pl.ds(dy, 8)].reshape(512, 3 * C)
                        for pair in range(2)
                    ],
                    axis=0,
                )
                for u in range(4)
            ]
            sums = jnp.dot(
                cot_t[...], jnp.concatenate(rows, axis=1), preferred_element_type=F32
            )
            for tap in range(9):
                at = tap * C
                total = sums[:C, at : at + C] + sums[C:, at + 3 * C : at + 4 * C]
                part[dy, at : at + C] = total.astype(BF16).T
            swap(dy).start()

        @pl.when(dy > 0)
        def _():
            halve(dy - 1)

        return carry

    lax.fori_loop(0, 4, tap_row, 0)

    def decode(pair):
        total = convolve(shifts, big2, pair)
        for j in range(2):
            for xh in range(4):
                for half_x in range(2):
                    x = 2 * xh + half_x
                    piece = total[xh, :, j, :, half_x * C : half_x * C + C].reshape(64, C)
                    block = 2 * pair + j
                    dec_ref[block, x] = (piece + field[BLK + block, x].astype(F32)).astype(BF16)

    def x_moves(group):
        return [
            remote(
                piece_x.at[group, rep],
                piece_x.at[group, rep],
                x_sems.at[0],
                x_sems.at[1 + group],
                at_rep(rep_peer(step)),
            )
            for step in range(1, reps)
        ]

    def reduce_piece(group):
        @pl.when(chip < active)
        def _():
            drain(piece_in.at[group, 0 : chips - 1], plane_sems.at[1 + group])
            piece_in[group, chip] = half[group, piece_at(chip)]

            def add(index, total):
                return total + piece_in[group, index].astype(F32)

            total = lax.fori_loop(0, chips, add, jnp.zeros((piece_rows, C), F32))
            piece_x[group, rep] = total.astype(BF16)
            for move in x_moves(group):
                move.start()

    def spread_piece(group):
        @pl.when(chip < active)
        def _():
            drain(piece_x.at[group, 0 : reps - 1], x_sems.at[1 + group])
            total = piece_x[group, 0].astype(F32)
            for index in range(1, reps):
                total = total + piece_x[group, index].astype(F32)
            piece_own[group] = total.astype(BF16)

            def start(step):
                gather(group, step).start()

            each_step(start)
            pltpu.make_async_copy(
                piece_own.at[group],
                grad_ref.at[final_at(group, core, chip)],
                load_sems.at[9 + group],
            ).start()
            forward(group, chip, piece_own.at[group]).start()

    def forward_pieces(group):
        if group < 2:

            @pl.when(chip < active)
            def _():
                drain(piece_in.at[group, 0 : active - 1], gather_sems.at[1 + group])

            @pl.when(chip >= active)
            def _():
                drain(piece_in.at[group, 0:active], gather_sems.at[1 + group])

        def come(step):
            @pl.when(from_chip(step) < active)
            def _():
                if group == 2:
                    drain(piece_own.at[group], gather_sems.at[2 + step])
                forward(group, from_chip(step)).start()

        each_step(come)

    def finish():
        drain(half_in, forward_sems.at[1])
        drain(half_in, forward_sems.at[0])
        drain(arrived_label.at[0 : peers - 1], label_sems.at[0])
        drain(arrived.at[0 : peers - 1], tile_sems.at[0])
        drain(pooled.at[0:3], sibling_sems.at[0])
        shell_drain(encoded, ends2_in, encoded_sems, 0)
        drain(half_in, core_sems.at[0])

        @pl.when(chip < active)
        def _():
            drain(piece_in.at[:, 0 : active - 1], plane_sems.at[0])
            drain(piece_x.at[:, 0 : reps - 1], x_sems.at[0])
            drain(piece_in.at[:, 0 : chips - 1], gather_sems.at[0])
            for group in range(3):
                drain(piece_own.at[group], load_sems.at[9 + group])

        @pl.when(chip >= active)
        def _():
            drain(piece_in.at[:, 0:active], plane_sems.at[0])

    decode(0)
    reduce_piece(0)
    reduce_piece(1)
    decode(1)
    reduce_piece(2)
    spread_piece(0)
    spread_piece(1)
    spread_piece(2)
    for group in range(3):
        forward_pieces(group)
    finish()


def local(
    peers,
    reps,
    tiles,
    tile_rows,
    tile_owner,
    tile_slot,
    neighbors,
    w_enc,
    w_coarse,
    w_dec,
    cotangent,
):
    count = tiles.shape[1]
    chips = peers // 2
    group_half = 9 * C // 2
    piece_rows = min(
        rows for rows in (16, 48, 64, 192, 576) if rows * chips >= group_half
    )
    vmem = pl.BlockSpec(memory_space=pltpu.VMEM)
    anywhere = pl.BlockSpec(memory_space=pltpu.HBM)
    dma = pltpu.SemaphoreType.DMA
    decoded, grads = pl.pallas_call(
        functools.partial(kernel, count, peers, reps),
        out_shape=(
            jax.ShapeDtypeStruct((BLK, 8, 64, C), BF16),
            jax.ShapeDtypeStruct((27 * C, C), BF16),
        ),
        in_specs=[anywhere] * 6 + [vmem] + [anywhere] * 2,
        out_specs=(vmem, anywhere),
        scratch_shapes=[
            pltpu.SMEM((1, count), jnp.int32),
            pltpu.SMEM((1, count), jnp.int32),
            pltpu.SMEM((1, count), jnp.int32),
            pltpu.SMEM((BLK, 27), jnp.int32),
            pltpu.SMEM((BLK * 27,), jnp.int32),
            pltpu.VMEM((8, C), jnp.int32),
            pltpu.SMEM((8, C), jnp.int32),
            pltpu.VMEM((count, C, C), BF16),
            pltpu.VMEM((peers, CAP, C, C), BF16),
            pltpu.VMEM((peers, CAP, C), jnp.int32),
            pltpu.VMEM((peers, CAP, C, C), BF16),
            pltpu.VMEM((peers, CAP, C), jnp.int32),
            pltpu.VMEM((4 * BLK, C, C), F32),
            pltpu.VMEM((3 * BLK + 1, 8, 64, C), BF16),
            pltpu.VMEM((3 * BLK, 8, 64, C), BF16),
            pltpu.VMEM((2, 2, 5, 10, 16, 3 * C), BF16),
            pltpu.VMEM((12, 3 * C, 2 * C), BF16),
            pltpu.VMEM((12, 3 * C, 2 * C), BF16),
            pltpu.VMEM((27, C, C), BF16),
            pltpu.VMEM((27, C, C), BF16),
            pltpu.VMEM((BLK, 8, 64, C), BF16),
            pltpu.VMEM((2 * C, 1024), BF16),
            pltpu.VMEM((SIB, BLK, 4, 16, C), BF16),
            pltpu.VMEM((3, BLK, 4, 16, C), BF16),
            pltpu.VMEM((3, 9 * C, C), BF16),
            pltpu.VMEM((3, group_half, C), BF16),
            pltpu.VMEM((3, group_half, C), BF16),
            pltpu.VMEM((3, chips, piece_rows, C), BF16),
            pltpu.VMEM((3, reps, piece_rows, C), BF16),
            pltpu.VMEM((3, piece_rows, C), BF16),
            pltpu.VMEM((BLK, 48, C), BF16),
            pltpu.VMEM((2, BLK, 48, C), BF16),
            pltpu.VMEM((BLK, 48, C), BF16),
            pltpu.VMEM((2, BLK, 48, C), BF16),
            dma((12,)),
            dma((peers,)),
            dma((peers,)),
            dma((6,)),
            dma((6,)),
            dma((5,)),
            dma((2,)),
            dma((4,)),
            dma((4,)),
            dma((4,)),
            dma((2 + chips,)),
            dma((2,)),
        ],
        compiler_params=pltpu.CompilerParams(
            collective_id=0, has_side_effects=True, vmem_limit_bytes=VMEM_LIMIT
        ),
        name="level",
    )(
        *[
            pltpu.with_memory_space_constraint(operand, pltpu.HBM)
            for operand in (
                tile_rows,
                tile_owner.reshape(1, count),
                tile_slot,
                neighbors[0],
                tiles[0],
                w_enc,
                w_coarse,
                w_dec,
                cotangent[0].reshape(BLK, 8, 64, C),
            )
        ]
    )
    return decoded.reshape(1, BLK, 512, C), grads.astype(F32).reshape(27, C, C)


def solution(mesh):
    placed = (
        P("rep", "blk", None, None),
        P("rep", "blk"),
        P("rep", "blk", None),
        P("rep", "blk"),
        P("rep", "blk", None),
        P(),
        P(),
        P(),
        P("rep", "blk", None, None),
    )
    return jax.shard_map(
        functools.partial(local, mesh.shape["blk"], mesh.shape["rep"]),
        mesh=mesh,
        in_specs=placed,
        out_specs=(P("rep", "blk", None, None), P()),
        check_vma=False,
    )
```

profile of v0, /device:TPU:1, one launch (start us, length us, event | category | flops | bytes accessed | tf_op | source)
XLA Modules:
  0.0 85.7 jit_solution(12928118033650615090)
XLA Ops:
  0.6 82.9 %level.1 = (bf16[4,8,64,128]{3,2,1,0:T(8,128)(2,1)S(1)}, bf16[3456,128]{1,0:T(8,128)(2,1)S(1)}) custom-call(s32[1,32]{1,0:T(1,128)} %rows_hbm.1, s32[1,32]{1,0:T(1,128)} %bitcast.12, s32[1,32]{1,0:T(1,128)} %slot_hbm.1, s32[4,27]{1,0:T(4,128)} %bitcast.11, bf16[32,128,128]{2,1,0:T(8,128)(2,1)} %bitcast.9, bf16[27,128,128]{2,1,0:T(8,128)(2,1)} %wenc_hbm.1, ...), custom_call_target="tpu_custom_call" | custom-call | tf_op jit(solution)/shard_map/level/pallas_call | solution.py:785
  83.5 1.4 %convert.1 = f32[27,128,128]{2,1,0:T(8,128)} convert(bf16[27,128,128]{2,1,0:T(8,128)(2,1)S(1)} %bitcast.7) | non-fusion elementwise | flops 442368 | bytes 2654208 | tf_op jit(solution)/shard_map/reshape | solution.py:861
  84.9 0.8 copy.12
where the time goes:
time: 85.9 us; the launch traced here: 85.7 us
  Pallas kernels  82.9 us (97%)
  other arithmetic  1.41 us (2%)
    pallas_call x1, Pallas kernels, local(): pl.pallas_call(functools.partial(kernel, count, peers, reps), out_shape=(...  82.9 us

commit v1 on v0

--- a/solution.py
+++ b/solution.py
@@ -121,6 +121,7 @@
     cot,
     cot_t,
     pooled,
+    sums,
     means,
     part,
     half_in,
@@ -138,7 +139,6 @@
     halo_sems,
     encoded_sems,
     sibling_sems,
-    mean_sems,
     core_sems,
     plane_sems,
     x_sems,
@@ -387,10 +387,10 @@
                 )
         return moves
 
-    def row_moves(ref, sems):
+    def row_moves(ref, first, count, sems):
         moves = []
         for base, where in ((0, right), (2 * BLK, left)):
-            source, target = pl.ds(BLK, BLK), pl.ds(base, BLK)
+            source, target = pl.ds(BLK + first, count), pl.ds(base + first, count)
             for y in (0, 48):
                 at = pl.ds(y, 16)
                 moves.append(
@@ -415,7 +415,7 @@
         drain(ref.at[0 : 2 * BLK, 1:7, 0:32], sems.at[2 + which])
         drain(ends_in, sems.at[4 + which])
 
-    for move in plane_moves(field, 0, BLK, halo_sems) + row_moves(field, halo_sems):
+    for move in plane_moves(field, 0, BLK, halo_sems) + row_moves(field, 0, BLK, halo_sems):
         move.start()
 
     def pack_own(block, carry):
@@ -433,14 +433,41 @@
     level = lax.broadcasted_iota(jnp.int32, (8, C), 0)
     even = lax.rem(level, 2) == 0
 
-    def sibling_move(pair, where, kind):
-        piece = pooled.at[turn, pl.ds(2 * pair, 2)]
+    in_group = turn // 2
+    base = me - turn
+    beyond = lax.rem(base + jnp.where(core == 0, peers - 1, SIB), peers)
+
+    def swap_pooled(pair):
+        piece = pooled.at[core, pl.ds(2 * pair, 2)]
         return remote(
-            piece, piece, sibling_sems.at[0], sibling_sems.at[1 + kind], at_blk(where)
-        )
+            piece, piece, sibling_sems.at[0], sibling_sems.at[1 + pair], at_blk(other)
+        )
+
+    def sum_chip(pair):
+        at = pl.ds(2 * pair, 2)
+        drain(pooled.at[0, 0:2], sibling_sems.at[1 + pair])
+        sums[2 + in_group, at] = (
+            pooled[0, at].astype(F32) + pooled[1, at].astype(F32)
+        ).astype(BF16)
+        source = sums.at[2 + in_group, at]
+        remote(
+            source, source, sibling_sems.at[0], sibling_sems.at[3 + pair], at_blk(across)
+        ).start()
+        remote(
+            source,
+            sums.at[4 * (1 - core) + in_group, at],
+            sibling_sems.at[0],
+            sibling_sems.at[5],
+            at_blk(beyond),
+        ).start()
 
     def encode(pair, carry):
         total = convolve(shifts, big, pair)
+
+        @pl.when(pair == 1)
+        def _():
+            sum_chip(0)
+
         rounded = jnp.maximum(total, 0.0).astype(BF16).astype(F32)
         for j in range(2):
             for xh in range(4):
@@ -461,15 +488,14 @@
                 packed = [
                     jnp.where(even, folded[2 * y], folded[2 * y + 1]) * 0.125 for y in range(2)
                 ]
-                pooled[turn, 2 * pair + j, xh] = jnp.concatenate(packed, axis=0).astype(BF16)
-        sibling_move(pair, across, pair).start()
-        sibling_move(pair, other, 2).start()
+                pooled[core, 2 * pair + j, xh] = jnp.concatenate(packed, axis=0).astype(BF16)
+        swap_pooled(pair).start()
         for move in plane_moves(encoded, 2 * pair, 2, encoded_sems):
             move.start()
 
-        @pl.when(pair == 1)
+        @pl.when(pair == 0)
         def _():
-            for move in row_moves(encoded, encoded_sems):
+            for move in row_moves(encoded, 0, 2, encoded_sems):
                 move.start()
 
         for j in range(2):
@@ -477,40 +503,17 @@
         return carry
 
     lax.fori_loop(0, 2, encode, 0)
-    for move in ends_moves(ends2, ends2_in, encoded_sems):
+    sum_chip(1)
+    for move in row_moves(encoded, 2, 2, encoded_sems) + ends_moves(ends2, ends2_in, encoded_sems):
         move.start()
 
-    opposite = lax.rem(turn + 2, SIB)
+    def mean_of(group):
+        total = sums[2 * group].astype(F32) + sums[2 * group + 1].astype(F32)
+        means[group] = (total * (1.0 / SIB)).astype(BF16)
+
     for pair in range(2):
-        piece = pooled.at[opposite, 2 * pair : 2 * pair + 2]
-        drain(piece, sibling_sems.at[1 + pair])
-        remote(piece, piece, sibling_sems.at[0], sibling_sems.at[4], at_blk(other)).start()
-    drain(pooled.at[0], sibling_sems.at[3])
-    drain(pooled.at[0], sibling_sems.at[4])
-    mean = pooled[0].astype(F32)
-    for step in range(1, SIB):
-        mean = mean + pooled[step].astype(F32)
-    means[1] = (mean * (1.0 / SIB)).astype(BF16)
-
-    def mean_move(side_of, where):
-        return remote(
-            means.at[1], means.at[side_of], mean_sems.at[0], mean_sems.at[1], at_blk(where)
-        )
-
-    @pl.when(turn == SIB - 1)
-    def _():
-        mean_move(0, right).start()
-        means[0] = means[1]
-
-    @pl.when(turn == 0)
-    def _():
-        mean_move(2, left).start()
-        means[2] = means[1]
-
-    @pl.when((turn != 0) & (turn != SIB - 1))
-    def _():
-        means[0] = means[1]
-        means[2] = means[1]
+        drain(pooled.at[0, 0:2], sibling_sems.at[3 + pair])
+    mean_of(1)
 
     def join(side_of):
         coarse = jnp.dot(
@@ -535,10 +538,20 @@
 
     join(1)
 
+    means[0] = means[1]
+    means[2] = means[1]
+
     @pl.when((turn == 0) | (turn == SIB - 1))
     def _():
-        drain(means.at[1], mean_sems.at[0])
-        drain(means.at[1], mean_sems.at[1])
+        drain(sums.at[0:2], sibling_sems.at[5])
+
+    @pl.when(turn == 0)
+    def _():
+        mean_of(0)
+
+    @pl.when(turn == SIB - 1)
+    def _():
+        mean_of(2)
 
     shell_drain(encoded, ends2_in, encoded_sems, 1)
     unpack_ends(ends2_in, encoded)
@@ -633,12 +646,12 @@
                 )
                 for u in range(4)
             ]
-            sums = jnp.dot(
+            taps = jnp.dot(
                 cot_t[...], jnp.concatenate(rows, axis=1), preferred_element_type=F32
             )
             for tap in range(9):
                 at = tap * C
-                total = sums[:C, at : at + C] + sums[C:, at + 3 * C : at + 4 * C]
+                total = taps[:C, at : at + C] + taps[C:, at + 3 * C : at + 4 * C]
                 part[dy, at : at + C] = total.astype(BF16).T
             swap(dy).start()
 
@@ -731,7 +744,7 @@
         drain(half_in, forward_sems.at[0])
         drain(arrived_label.at[0 : peers - 1], label_sems.at[0])
         drain(arrived.at[0 : peers - 1], tile_sems.at[0])
-        drain(pooled.at[0:3], sibling_sems.at[0])
+        drain(sums.at[0:3], sibling_sems.at[0])
         shell_drain(encoded, ends2_in, encoded_sems, 0)
         drain(half_in, core_sems.at[0])
 
@@ -813,7 +826,8 @@
             pltpu.VMEM((27, C, C), BF16),
             pltpu.VMEM((BLK, 8, 64, C), BF16),
             pltpu.VMEM((2 * C, 1024), BF16),
-            pltpu.VMEM((SIB, BLK, 4, 16, C), BF16),
+            pltpu.VMEM((2, BLK, 4, 16, C), BF16),
+            pltpu.VMEM((6, BLK, 4, 16, C), BF16),
             pltpu.VMEM((3, BLK, 4, 16, C), BF16),
             pltpu.VMEM((3, 9 * C, C), BF16),
             pltpu.VMEM((3, group_half, C), BF16),
@@ -830,8 +844,7 @@
             dma((peers,)),
             dma((6,)),
             dma((6,)),
-            dma((5,)),
-            dma((2,)),
+            dma((6,)),
             dma((4,)),
             dma((4,)),
             dma((4,)),

time: 85.9 us -> 85.5 us (level)
  no operation moved by 1% of the time
where the time goes in v1:
time: 85.5 us; the launch traced here: 85.4 us
  Pallas kernels  82.5 us (96%)
  other arithmetic  1.41 us (2%)
    pallas_call x1, Pallas kernels, local(): pl.pallas_call(functools.partial(kernel, count, peers, reps), out_shape=(...  82.5 us

profile of v1, /device:TPU:1, one launch (start us, length us, event | category | flops | bytes accessed | tf_op | source)
XLA Modules:
  0.0 85.4 jit_solution(13647489409388489862)
XLA Ops:
  0.6 82.5 %level.1 = (bf16[4,8,64,128]{3,2,1,0:T(8,128)(2,1)S(1)}, bf16[3456,128]{1,0:T(8,128)(2,1)S(1)}) custom-call(s32[1,32]{1,0:T(1,128)} %rows_hbm.1, s32[1,32]{1,0:T(1,128)} %bitcast.12, s32[1,32]{1,0:T(1,128)} %slot_hbm.1, s32[4,27]{1,0:T(4,128)} %bitcast.11, bf16[32,128,128]{2,1,0:T(8,128)(2,1)} %bitcast.9, bf16[27,128,128]{2,1,0:T(8,128)(2,1)} %wenc_hbm.1, ...), custom_call_target="tpu_custom_call" | custom-call | tf_op jit(solution)/shard_map/level/pallas_call | solution.py:798
  83.1 1.4 %convert.1 = f32[27,128,128]{2,1,0:T(8,128)} convert(bf16[27,128,128]{2,1,0:T(8,128)(2,1)S(1)} %bitcast.7) | non-fusion elementwise | flops 442368 | bytes 2654208 | tf_op jit(solution)/shard_map/reshape | solution.py:874
  84.6 0.8 copy.12

commit v2 on v1

--- a/solution.py
+++ b/solution.py
@@ -16,6 +16,8 @@
 BF16 = jnp.bfloat16
 MESH = pl.DeviceIdType.MESH
 WINDOW = 16
+MOVES_Y = (1, 1, 2, 1, 0, 2, 1, 3, 3, 2, 0, 2, 3, 3, 0)
+MOVES_Z = (1, 3, 2, 0, 1, 1, 2, 1, 3, 0, 2, 3, 2, 0, 3)
 VMEM_LIMIT = 48 * 1024 * 1024
 
 
@@ -237,19 +239,33 @@
             outgoing[owner, rank] = jnp.where(row < live, tiles[at].astype(F32), 0.0).astype(BF16)
             outgoing_label[owner, rank : rank + 1] = jnp.full((1, C), slot_s[0, at], jnp.int32)
 
+    def pick(table, k):
+        value = 0
+        for at, entry in enumerate(table):
+            value = jnp.where(k == at, entry, value)
+        return value
+
     def chip_beside(step, sign):
-        k = step // 2
-        move_y = lax.rem(k, side)
-        move_z = lax.rem(k // side + move_y, side)
+        k = lax.rem(step - 1, chips - 1)
+        if side == 4:
+            move_y, move_z = pick(MOVES_Y, k), pick(MOVES_Z, k)
+        else:
+            move_y = lax.rem(k + 1, side)
+            move_z = lax.rem((k + 1) // side + move_y, side)
+        away = step < peers - 1
+        move_y, move_z = jnp.where(away, move_y, 0), jnp.where(away, move_z, 0)
         return side * lax.rem(chip_z + side + sign * move_z, side) + lax.rem(
             chip_y + side + sign * move_y, side
         )
 
+    def turned(step):
+        return jnp.where(step < chips, core, 1 - core)
+
     def target_of(step):
-        return 2 * chip_beside(step, 1 - 2 * core) + lax.rem(core + step, 2)
+        return 2 * chip_beside(step, 1 - 2 * core) + turned(step)
 
     def source_of(step):
-        from_core = lax.rem(core + step, 2)
+        from_core = turned(step)
         return 2 * chip_beside(step, 2 * from_core - 1) + from_core
 
     def label_move(step):
@@ -271,7 +287,7 @@
     pl.semaphore_wait(barrier, peers - 1 + reps - 1)
 
     def step_of(i):
-        return 1 + lax.rem(i + 1, peers - 1)
+        return 1 + i
 
     def send(i, carry):
         step = step_of(i)

time: 85.5 us -> 84.5 us (0.988)
  Pallas kernels: 82.5 us -> 81.4 us
    pallas_call x1, Pallas kernels: 82.5 us -> 81.4 us  [local(): pl.pallas_call(functools.partial(kernel, count, peers, reps), out_shape=(...]
where the time goes in v2:
time: 84.5 us; the launch traced here: 84.3 us
  Pallas kernels  81.4 us (96%)
  other arithmetic  1.41 us (2%)
    pallas_call x1, Pallas kernels, local(): pl.pallas_call(functools.partial(kernel, count, peers, reps), out_shape=(...  81.4 us

profile of v2, /device:TPU:1, one launch (start us, length us, event | category | flops | bytes accessed | tf_op | source)
XLA Modules:
  0.0 84.3 jit_solution(2530312960068734700)
XLA Ops:
  0.6 81.4 %level.1 = (bf16[4,8,64,128]{3,2,1,0:T(8,128)(2,1)S(1)}, bf16[3456,128]{1,0:T(8,128)(2,1)S(1)}) custom-call(s32[1,32]{1,0:T(1,128)} %rows_hbm.1, s32[1,32]{1,0:T(1,128)} %bitcast.12, s32[1,32]{1,0:T(1,128)} %slot_hbm.1, s32[4,27]{1,0:T(4,128)} %bitcast.11, bf16[32,128,128]{2,1,0:T(8,128)(2,1)} %bitcast.9, bf16[27,128,128]{2,1,0:T(8,128)(2,1)} %wenc_hbm.1, ...), custom_call_target="tpu_custom_call" | custom-call | tf_op jit(solution)/shard_map/level/pallas_call | solution.py:814
  82.1 1.4 %convert.1 = f32[27,128,128]{2,1,0:T(8,128)} convert(bf16[27,128,128]{2,1,0:T(8,128)(2,1)S(1)} %bitcast.7) | non-fusion elementwise | flops 442368 | bytes 2654208 | tf_op jit(solution)/shard_map/reshape | solution.py:890
  83.5 0.8 copy.12

commit v3 on v2

--- a/solution.py
+++ b/solution.py
@@ -15,7 +15,7 @@
 F32 = jnp.float32
 BF16 = jnp.bfloat16
 MESH = pl.DeviceIdType.MESH
-WINDOW = 16
+WINDOW = 20
 MOVES_Y = (1, 1, 2, 1, 0, 2, 1, 3, 3, 2, 0, 2, 3, 3, 0)
 MOVES_Z = (1, 3, 2, 0, 1, 1, 2, 1, 3, 0, 2, 3, 2, 0, 3)
 VMEM_LIMIT = 48 * 1024 * 1024

time: 84.5 us -> 84.6 us (level)
  no operation moved by 1% of the time
where the time goes in v3:
time: 84.6 us; the launch traced here: 84.4 us
  Pallas kernels  81.5 us (96%)
  other arithmetic  1.41 us (2%)
    pallas_call x1, Pallas kernels, local(): pl.pallas_call(functools.partial(kernel, count, peers, reps), out_shape=(...  81.5 us

profile of v3, /device:TPU:1, one launch (start us, length us, event | category | flops | bytes accessed | tf_op | source)
XLA Modules:
  0.0 84.4 jit_solution(11164448887460516575)
XLA Ops:
  0.6 81.5 %level.1 = (bf16[4,8,64,128]{3,2,1,0:T(8,128)(2,1)S(1)}, bf16[3456,128]{1,0:T(8,128)(2,1)S(1)}) custom-call(s32[1,32]{1,0:T(1,128)} %rows_hbm.1, s32[1,32]{1,0:T(1,128)} %bitcast.12, s32[1,32]{1,0:T(1,128)} %slot_hbm.1, s32[4,27]{1,0:T(4,128)} %bitcast.11, bf16[32,128,128]{2,1,0:T(8,128)(2,1)} %bitcast.9, bf16[27,128,128]{2,1,0:T(8,128)(2,1)} %wenc_hbm.1, ...), custom_call_target="tpu_custom_call" | custom-call | tf_op jit(solution)/shard_map/level/pallas_call | solution.py:814
  82.2 1.4 %convert.1 = f32[27,128,128]{2,1,0:T(8,128)} convert(bf16[27,128,128]{2,1,0:T(8,128)(2,1)S(1)} %bitcast.7) | non-fusion elementwise | flops 442368 | bytes 2654208 | tf_op jit(solution)/shard_map/reshape | solution.py:890
  83.6 0.8 copy.12
